TPU v7x, 32 devices: a whole 2x2x4 slice. The times are simulated.
32 devices in a mesh: batch: 4 (over y, x), mp: 8 (over z, core).
Axes of the slice: x: 2, y: 2, z: 4, core: 2. Of those that a mesh axis runs over, the one named last changes fastest.
Arguments:
- pool_in: bfloat16 [2, 2048, 9216], P(None, 'batch', 'mp'), may hold values from -6 to 6
- weights: bfloat16 [2, 9216, 4096], P(None, None, 'mp'), may hold values from -0.0625 to 0.0625
- bias: float32 [2, 4096], P(None, 'mp'), may hold values from -3 to 3
- stitch: float32 [2, 2, 4096], P(None, None, 'mp')
- crops: int32 [512], P('batch'), may hold values from 1 to 4, as said below
- row_mask: int32 [2048], P('batch'), may hold values 0 or 1
- cotangent: bfloat16 [2, 2048, 4096], P(None, 'batch', 'mp'), may hold values from -6 to 6
Outputs:
- mixed: bfloat16 [2, 2048, 4096], P(None, 'batch')
- input_grad: bfloat16 [2, 2048, 9216], P(None, 'batch', 'mp')
- weight_grad: float32 [2, 9216, 4096], P(None, None, 'mp')
- bias_grad: float32 [2, 4096], P(None, 'mp')
- stitch_grad: float32 [2, 2, 4096], P(None, None, 'mp')
Inputs may be any that keep to these rules, and one draw needn't show every extreme that they name: crops of the images of each batch shard; every shard has an image of one crop.
All inputs are finite; a program needn't handle non-finite values. No bound on the sum of `row_mask` on one device may be relied on, other than what follows from the above.
Results may differ from a plain program's by a relative error of at most 0.005.
Values may be sent and summed in bfloat16 or wider, within the bound.
A program may use at most 320 MiB of HBM per device.

v0:
```python
import functools

import jax
import jax.numpy as jnp
from jax import lax
from jax.experimental import pallas as pl
from jax.experimental.pallas import tpu as pltpu
from jax.sharding import PartitionSpec as P

MESH = pl.DeviceIdType.MESH
F32 = jnp.float32
BF16 = jnp.bfloat16
LAYERS = 4
GROUP = 4
TASKS = 2
TANH_SCALE = 0.7978845608
TANH_CUBE = 0.044715

CORNER_LATER = ((1, 2), (1, 3))
HALVED = ()
VIA_LAYERS = ((0, 0), (0, 3))
ORDER = (
    ("share", 0, 0), ("own", 0), ("share", 1, 0), ("layer", 0, 1), ("square", 0, 0), ("share", 0, 1), ("layer", 0, 2),
    ("forward", 0, 0), ("share", 0, 2), ("own", 1), ("forward", 0, 1), ("layer", 0, 3), ("forward", 0, 2),
    ("corner", 0, 0), ("forward", 0, 3), ("activate", 0), ("core_terms", 0), ("layer", 1, 1), ("square", 0, 1),
    ("square", 1, 0), ("chain", 0, 0), ("layer", 1, 2), ("square", 0, 2), ("forward", 1, 2), ("forward", 1, 1),
    ("chain", 0, 1), ("dpre", 0), ("corner", 0, 1), ("share", 1, 1), ("chain", 0, 2), ("forward", 1, 0),
    ("layer", 1, 3), ("share", 0, 3), ("forward", 1, 3), ("activate", 1), ("gradient", 0, 1), ("corner", 0, 2),
    ("share", 1, 2), ("chain", 0, 3), ("core_terms", 1), ("gradient", 0, 0), ("chain", 1, 0), ("mixed", 1),
    ("gradient", 0, 2), ("dpre", 1), ("corner", 1, 0), ("square", 0, 3), ("corner", 0, 3), ("places",),
    ("share", 1, 3), ("square", 1, 1), ("gradient", 0, 3), ("chain", 1, 1), ("square", 1, 2), ("gradient", 1, 0),
    ("square", 1, 3), ("chain", 1, 2), ("mixed", 2), ("gradient", 1, 2), ("gradient", 1, 3), ("corner", 1, 1),
    ("corner", 1, 2), ("chain", 1, 3), ("gradient", 1, 1), ("mixed", 3), ("corner", 1, 3),
)


def row_weights(crops, row_mask):
    slots = jnp.arange(row_mask.shape[0], dtype=jnp.int32)
    ends = jnp.cumsum(crops)
    image = jnp.sum((slots[:, None] >= ends[None, :]).astype(jnp.int32), axis=1)
    inside = slots < ends[-1]
    onehot = (image[:, None] == jnp.arange(crops.shape[0], dtype=jnp.int32)[None, :]).astype(
        jnp.int32
    )
    count = jnp.sum(onehot * crops[None, :], axis=1)
    count = jnp.where(inside, count, 1).astype(jnp.float32)
    valid = (row_mask * inside.astype(jnp.int32)).astype(jnp.float32)
    return (count, valid)


def exchange(pool, w, bias, stitch, crops, mask, first, cotangent, xg, dg, mg, ig, st, place, wg, at,
             wv, pre, dpv, mxv, gx, xc, cot, dgv, dgt, gout, scale, acc, sbuf, rup, rdn, tso, tsi, stv,
             wsem, lsem, osem, z_r, z_u, z_d, o_x, o_y, r_x, r_y, r_d, f_s, c_r, c_s,
             dp_s, dp_r, m_r, m_u, m_d, mc_r, mc_s, t_u, t_d, t_s, tc_r, tc_s, st_s, st_r, ig_s, go_s, v_u, v_d, f_h, r_h):
    rows, depth = xc.shape[1], xc.shape[2]
    cols, slots, images = w.shape[2], mask.shape[1], crops.shape[1]
    b, m = lax.axis_index("batch"), lax.axis_index("mp")
    z, c = m // 2, m % 2
    y, x = b // 2, b % 2
    bx, by, bd = y * 2 + (1 - x), (1 - y) * 2 + x, 3 - b
    to_x, to_y, to_d = (bx, m), (by, m), (bd, m)
    to_c = (b, z * 2 + 1 - c)
    up, down = (b, m + 2), (b, m - 2)
    not_top, not_bottom = z < LAYERS - 1, z > 0
    everyone = [(None, to_x), (None, to_y), (None, to_d), (None, to_c), (not_top, up), (not_bottom, down)]

    barrier = pltpu.get_barrier_semaphore()
    for cond, dev in everyone:
        def greet(dev=dev):
            pl.semaphore_signal(barrier, inc=1, device_id=dev, device_id_type=MESH)
        greet() if cond is None else pl.when(cond)(greet)
    drains = []
    lent = {}

    def give_back(name):
        for drain in lent.pop(name, ()):
            drain()

    def remote(src, dst, send, recv, dev):
        return pltpu.make_async_remote_copy(
            src_ref=src, dst_ref=dst, send_sem=send, recv_sem=recv, device_id=dev, device_id_type=MESH)

    def send(src, dst, ssem, rsem, dev, cond=None):
        def go():
            remote(src, dst, ssem, rsem, dev).start()
        def drain():
            remote(src, dst, ssem, rsem, dev).wait_send()
        if cond is None:
            go()
            drains.append(drain)
        else:
            pl.when(cond)(go)
            drains.append(lambda: pl.when(cond)(drain))

    def arrived(dst, rsem, cond=None):
        def go():
            remote(dst, dst, rsem, rsem, to_c).wait_recv()
        go() if cond is None else pl.when(cond)(go)

    def local(src, dst, sem):
        copy = pltpu.make_async_copy(src, dst, sem)
        copy.start()
        drains.append(copy.wait)
        return copy

    def span(who):
        return pl.ds(pl.multiple_of(who * rows, 16), rows)

    top = (rows // 2 + 15) // 16 * 16
    outer = (z == 0) | (z == LAYERS - 1)
    inner = jnp.logical_not(outer)

    def slot(t, layer, plane, who, half=None):
        part = span(who)
        if half is not None:
            part = pl.ds(pl.multiple_of(who * rows + half * top, 16), rows - top if half else top)
        return xg.at[layer * 2 + plane, t, part, :]

    load_w = pltpu.make_async_copy(w, wv, wsem)
    load_pool = [pltpu.make_async_copy(pool.at[t], gx.at[t, pl.ds(0, slots), :], lsem.at[t]) for t in range(TASKS)]

    def grid(shape, axis):
        return lax.broadcasted_iota(jnp.int32, shape, axis).astype(F32)

    def row_weights():
        square = (images, images)
        wide = jnp.broadcast_to(crops[...].astype(F32), square)
        lane, sub = grid(square, 1), grid(square, 0)
        end = jnp.sum(jnp.where(lane <= sub, wide, 0.0), axis=1, keepdims=True)
        crop = jnp.sum(jnp.where(lane == sub, wide, 0.0), axis=1, keepdims=True)
        at = grid((images, slots), 1)
        inside = jnp.where((at < end) & (at >= end - crop), 1.0, 0.0)
        count = jnp.sum(inside * crop, axis=0, keepdims=True)
        valid = mask[...].astype(F32) * jnp.sum(inside, axis=0, keepdims=True)
        return valid, valid / jnp.maximum(count, 1.0)

    def pack():
        valid, weight = row_weights()
        square = (slots, slots)
        upto = jnp.where(grid(square, 0) <= grid(square, 1), 1.0, 0.0).astype(BF16)
        many = jnp.broadcast_to(valid, (16, slots)).astype(BF16)
        index = jnp.dot(many, upto, preferred_element_type=F32)[0:1, :] - 1.0 - first[...].astype(F32)
        pick = jnp.where((grid((rows, slots), 0) == index) & (valid > 0.0), 1.0, 0.0)
        scale[...] = jnp.sum(pick * weight, axis=1, keepdims=True)
        stv[b, 6:7, :] = jnp.broadcast_to(jnp.sum(valid, axis=1, keepdims=True), (1, cols))
        stv[b, 7:8, :] = jnp.zeros((1, cols), F32)
        pick = pick.astype(BF16)
        for t in range(TASKS):
            load_pool[t].wait()
            xc[t] = jnp.dot(pick, gx[t, 0:slots, :], preferred_element_type=F32).astype(BF16)
        for t in range(TASKS):
            cot[t] = jnp.dot(pick, cotangent[t], preferred_element_type=F32).astype(BF16)

    def places():
        valid, _ = row_weights()
        square = (slots, slots)
        wide = jnp.broadcast_to(valid, square)
        lane, sub = grid(square, 1), grid(square, 0)
        index = jnp.sum(jnp.where(lane <= sub, wide, 0.0), axis=1, keepdims=True) - 1.0 - first[...].astype(F32)
        here = jnp.sum(jnp.where(lane == sub, wide, 0.0), axis=1, keepdims=True)
        place[...] = jnp.where((grid((slots, rows), 1) == index) & (here > 0.0), 1.0, 0.0).astype(BF16)

    own = [pltpu.make_async_copy(xc.at[t], slot(t, z, c, b), osem.at[t]) for t in range(TASKS)]

    def own_z(t):
        send(xc.at[t], slot(t, z, c, b), z_u.at[t, z], z_r.at[t, z], up, not_top)
        send(xc.at[t], slot(t, z, c, b), z_d.at[t, z], z_r.at[t, z], down, not_bottom)

    def to_core(t, src, layer, cond=None):
        send(src, slot(t, layer, c, b), c_s.at[0, t, layer], c_r.at[0, t, layer], to_c, cond)

    def to_square(t, src, layer, cond=None):
        send(src, slot(t, layer, c, b), o_x.at[t, layer], r_x.at[t, layer], to_x, cond)
        send(src, slot(t, layer, c, b), o_y.at[t, layer], r_y.at[t, layer], to_y, cond)

    def near(d):
        return [(z, None)] if d == 0 else [(z - d, z >= d), (z + d, z < LAYERS - d)]

    def z_step(t, d):
        (low, is_low), (high, is_high) = near(d)
        here = slot(t, low, c, b)
        arrived(here, z_r.at[t, low], is_low)
        send(here, here, z_u.at[t, low], z_r.at[t, low], up, is_low & not_top)
        to_core(t, here, low, is_low)
        there = slot(t, high, c, b)
        arrived(there, z_r.at[t, high], is_high)
        send(there, there, z_d.at[t, high], z_r.at[t, high], down, is_high & not_bottom)
        to_core(t, there, high, is_high)

    def square_sends(t, d):
        for layer, cond in near(d):
            to_square(t, xc.at[t] if d == 0 else slot(t, layer, c, b), layer, cond)

    def via_layers(t, layer):
        hit = [layer == chosen for task, chosen in VIA_LAYERS if task == t]
        return functools.reduce(lambda p, q: p | q, hit) if hit else None

    def square_step(t, d):
        for layer, cond in near(d):
            from_x, from_y = slot(t, layer, c, bx), slot(t, layer, c, by)
            even, odd = (t + layer) % 2 == 0, (t + layer) % 2 == 1
            if cond is not None:
                even, odd = even & cond, odd & cond
            if d > 0 and via_layers(t, layer) is not None:
                around = jnp.logical_not(via_layers(t, layer))
                even, odd = even & around, odd & around
            halved = (t, d) in HALVED
            if halved:
                even, odd = even & inner, odd & inner
            arrived(from_x, r_x.at[t, layer], cond)
            send(from_x, from_x, f_s.at[t, layer], r_d.at[t, layer], to_y, even)
            if halved:
                first = slot(t, layer, c, bx, 0)
                send(first, first, f_s.at[t, layer], r_d.at[t, layer], to_y, cond & outer)
            send(from_x, from_x, c_s.at[1, t, layer], c_r.at[1, t, layer], to_c, cond)
            arrived(from_y, r_y.at[t, layer], cond)
            send(from_y, from_y, f_s.at[t, layer], r_d.at[t, layer], to_x, odd)
            if halved:
                second = slot(t, layer, c, by, 1)
                send(second, second, f_h.at[t, layer], r_h.at[t, layer], to_x, cond & outer)
            send(from_y, from_y, c_s.at[2, t, layer], c_r.at[2, t, layer], to_c, cond)

    def corner_step(t, d):
        for layer, cond in near(d):
            from_d = slot(t, layer, c, bd)
            if (t, d) in HALVED:
                arrived(from_d, r_d.at[t, layer], cond & inner)
                arrived(slot(t, layer, c, bd, 0), r_d.at[t, layer], cond & outer)
                arrived(slot(t, layer, c, bd, 1), r_h.at[t, layer], cond & outer)
            else:
                arrived(from_d, r_d.at[t, layer], cond)
            on = via_layers(t, layer)
            if on is not None:
                send(from_d, from_d, v_u.at[t, layer], r_d.at[t, layer], up, on & (layer <= z) & not_top)
                send(from_d, from_d, v_d.at[t, layer], r_d.at[t, layer], down, on & (layer >= z) & not_bottom)
            send(from_d, from_d, c_s.at[3, t, layer], c_r.at[3, t, layer], to_c, cond)

    around = (b, bx, by, bd)

    def strip(i):
        return pl.ds(i * rows, rows)

    def forward(t, d):
        def add(mm, source):
            part = pl.ds(pl.multiple_of(mm * depth, 128), depth)

            def half(h, carry):
                out = pl.ds(pl.multiple_of(h * (cols // 2), 128), cols // 2)
                pre[t, :, out] += jnp.dot(source[...], wv[t, part, out], preferred_element_type=F32)
                return carry

            lax.fori_loop(0, 2, half, 0)

        def fetch(i, layer, plane):
            return pltpu.make_async_copy(
                xg.at[layer * 2 + plane, t, span(b), :], gx.at[plane, strip(i), :], lsem.at[i * 2 + plane])

        sides = near(d)
        if d == 0:
            own[t].wait()
        for i, (layer, cond) in enumerate(sides):
            def begin(i=i, layer=layer):
                arrived(slot(t, layer, 1 - c, b), c_r.at[0, t, layer])
                for plane in range(2):
                    fetch(i, layer, plane).start()
            begin() if cond is None else pl.when(cond)(begin)

        def block(n, carry):
            i, plane = n // 2, n % 2
            layer = z + (2 * i - 1) * d

            @pl.when((layer >= 0) & (layer < LAYERS))
            def _():
                pltpu.make_async_copy(
                    xg.at[layer * 2 + plane, t, span(b), :], gx.at[plane, pl.ds(pl.multiple_of(i * rows, 16), rows), :],
                    lsem.at[n]).wait()
                add(layer * 2 + plane, gx.at[plane, pl.ds(pl.multiple_of(i * rows, 16), rows), :])

            return carry

        lax.fori_loop(0, 2 * len(sides), block, 0)

    def fold(v):
        return jnp.sum(v.reshape(2, 8, v.shape[1]), axis=0)

    def activate(u):
        def chunk(i, sums):
            s0, s1, bb = sums
            part = pl.ds(pl.multiple_of(i * 16, 16), 16)
            v = pre[u, part, :]
            th = jnp.tanh(TANH_SCALE * (v + TANH_CUBE * (v * v * v)))
            h = 0.5 * v * (1.0 + th)
            slope = 0.5 * (1.0 + th) + 0.5 * v * (1.0 - th * th) * (TANH_SCALE * (1.0 + 3.0 * TANH_CUBE * (v * v)))
            sc = scale[part, :]
            g0 = cot[0, part, :].astype(F32) * sc
            g1 = cot[1, part, :].astype(F32) * sc
            dpre = (slope * (stitch[0, u:u + 1, :] * g0 + stitch[1, u:u + 1, :] * g1)).astype(BF16)
            dpv[u, part, :] = dpre
            if u == 0:
                pre[0, part, :] = h
            else:
                h0 = pre[0, part, :]
                for t in range(TASKS):
                    mxv[t, part, :] = (stitch[t, 0:1, :] * h0 + stitch[t, 1:2, :] * h).astype(BF16)
            return s0 + fold(g0 * h), s1 + fold(g1 * h), bb + fold(dpre.astype(F32))

        zero = jnp.zeros((8, cols), F32)
        s0, s1, bb = lax.fori_loop(0, rows // 16, chunk, (zero, zero, zero))
        stv[b, u:u + 1, :] = jnp.sum(s0, axis=0, keepdims=True)
        stv[b, 2 + u:3 + u, :] = jnp.sum(s1, axis=0, keepdims=True)
        stv[b, 4 + u:5 + u, :] = jnp.sum(bb, axis=0, keepdims=True)

    def spread_dpre(t):
        mine = dg.at[t, span(b), :]
        pltpu.make_async_copy(dpv.at[t], mine, dp_s.at[t, 3]).start()
        send(dpv.at[t], mine, dp_s.at[t, 0], dp_r.at[t, 0], to_x)
        send(dpv.at[t], mine, dp_s.at[t, 1], dp_r.at[t, 1], to_y)

    def forward_dpre(t):
        from_x, from_y = dg.at[t, span(bx), :], dg.at[t, span(by), :]
        arrived(from_x, dp_r.at[t, 0])
        arrived(from_y, dp_r.at[t, 1])
        if t == 0:
            send(from_x, from_x, dp_s.at[t, 2], dp_r.at[t, 2], to_y)
        else:
            send(from_y, from_y, dp_s.at[t, 2], dp_r.at[t, 2], to_x)

    def own_mixed():
        local(mxv, mg.at[m], mc_s.at[LAYERS])
        send(mxv, mg.at[m], m_u.at[z], m_r.at[z], up, not_top)
        send(mxv, mg.at[m], m_d.at[z], m_r.at[z], down, not_bottom)
        send(mxv, mg.at[m], mc_s.at[z], mc_r.at[z], to_c)

    def mixed_step(d):
        low, high = z - d, z + d
        here = mg.at[low * 2 + c]
        arrived(here, m_r.at[low], z >= d)
        send(here, here, m_u.at[low], m_r.at[low], up, (z >= d) & not_top)
        send(here, here, mc_s.at[low], mc_r.at[low], to_c, z >= d)
        there = mg.at[high * 2 + c]
        arrived(there, m_r.at[high], z < LAYERS - d)
        send(there, there, m_d.at[high], m_r.at[high], down, (z < LAYERS - d) & not_bottom)
        send(there, there, mc_s.at[high], mc_r.at[high], to_c, z < LAYERS - d)

    tiles = 3
    width = depth // tiles

    def lanes(j):
        return pl.ds(pl.multiple_of(j * width, 128), width)

    def term(t, mm, j):
        part = pl.ds(pl.multiple_of(mm * depth + j * width, 128), width)
        return lax.dot_general(dpv[t], wv[t, part, :], (((1,), (1,)), ((), ())), preferred_element_type=F32)

    def core_terms(t):
        def step(s, carry):
            part = pl.ds(pl.multiple_of((2 * s + 1 - c) * depth, 128), depth)
            tso[s] = lax.dot_general(
                dpv[t], wv[t, part, :], (((1,), (1,)), ((), ())), preferred_element_type=F32).astype(BF16)
            remote(tso.at[s], tsi.at[t, s], tc_s.at[t, s], tc_r.at[t, s], to_c).start()
            return carry

        lax.fori_loop(0, LAYERS, step, 0)
        lent["core"] = [lambda s=s: remote(
            tso.at[s], tsi.at[t, s], tc_s.at[t, s], tc_r.at[t, s], to_c).wait_send() for s in range(LAYERS)]

    def chain_step(t, k):
        s = [3 * (1 - z // 2), (2 + 3 * z) % 5, 1 + z % 2, z][k]
        has_up = (s >= z) & not_bottom
        has_down = (s <= z) & not_top
        give_back(k)
        arrived(tsi.at[t, s], tc_r.at[t, s])
        arrived(rup.at[t, s - 1], t_u.at[t, s], has_up)
        arrived(rdn.at[t, s], t_d.at[t, s], has_down)

        def step(j, carry):
            acc[...] = term(t, 2 * s + c, j) + tsi[t, s, :, lanes(j)].astype(F32)

            @pl.when(has_up)
            def _():
                acc[...] += rup[t, s - 1, :, lanes(j)].astype(F32)

            @pl.when(has_down)
            def _():
                acc[...] += rdn[t, s, :, lanes(j)].astype(F32)

            sbuf[s, :, lanes(j)] = acc[...].astype(BF16)
            return carry

        lax.fori_loop(0, tiles, step, 0)
        before = len(drains)
        if k < LAYERS - 1:
            send(sbuf.at[s], rup.at[t, s - 1], t_s.at[t, s], t_u.at[t, s], up, s > z)
            send(sbuf.at[s], rdn.at[t, s], t_s.at[t, s], t_d.at[t, s], down, s < z)
        else:
            local(sbuf.at[s], ig.at[t], ig_s.at[t])
        lent[k] = drains[before:]
        del drains[before:]

    def all_dpre(t):
        arrived(dg.at[t, span(bd), :], dp_r.at[t, 2])
        pltpu.make_async_copy(dpv.at[t], dg.at[t, span(b), :], dp_s.at[t, 3]).wait()
        loads = [pltpu.make_async_copy(dg.at[t, span(who), :], dgv.at[strip(i), :], lsem.at[i])
                 for i, who in enumerate(around)]
        for copy in loads:
            copy.start()
        for copy in loads:
            copy.wait()
        dgt[...] = dgv[...].T

    def all_pieces(t, layer, corner=True):
        for k, who in ((1, bx), (2, by), (3, bd)):
            if k < 3 or corner:
                arrived(slot(t, layer, 1 - c, who), c_r.at[k, t, layer])

    def corner_pieces(t, layer):
        arrived(slot(t, layer, 1 - c, bd), c_r.at[3, t, layer])

    def gradient(t, layer, corner):
        many = GROUP if corner else GROUP - 1

        def load(k):
            mm = 2 * layer + k
            return [pltpu.make_async_copy(xg.at[mm, t, span(who), :], gx.at[k, strip(i), :], lsem.at[k * GROUP + i])
                    for i, who in enumerate(around[:many])]

        def store(k):
            return pltpu.make_async_copy(gout.at[k], wg.at[t, 2 * layer + k], go_s.at[k])

        for k in range(2):
            for copy in load(k):
                copy.start()
        give_back("gradient")
        wide = 2 * 128
        whole = depth // wide * wide

        def multiply(k, part):
            gout[k, :, part] = jnp.dot(
                dgt[:, 0:many * rows], gx[k, 0:many * rows, part], preferred_element_type=F32).astype(BF16)

        def tile(k, carry):
            for i in range(many):
                pltpu.make_async_copy(
                    xg.at[2 * layer + k, t, span(around[i]), :], gx.at[k, strip(i), :], lsem.at[k * GROUP + i]).wait()

            def step(j, carry):
                multiply(k, pl.ds(pl.multiple_of(j * wide, 128), wide))
                return carry

            lax.fori_loop(0, whole // wide, step, 0)
            if whole < depth:
                multiply(k, slice(whole, depth))
            store(k).start()
            return carry

        lax.fori_loop(0, 2, tile, 0)
        lent["gradient"] = [store(k).wait for k in range(2)]

    def own_step(t):
        own[t].start()
        own_z(t)
        to_core(t, xc.at[t], z)

    def activate_step(t):
        activate(t)
        spread_dpre(t)
        if t == 1:
            own_mixed()
            send(stv.at[b], stv.at[b], st_s.at[0], st_r.at[0], to_x)
            send(stv.at[b], stv.at[b], st_s.at[1], st_r.at[1], to_y)
            send(stv.at[b], stv.at[b], st_s.at[2], st_r.at[2], to_d)

    def core_step(t):
        give_back("core")
        core_terms(t)

    ready = []

    def nearest(j):
        return [z, z + 1 - 2 * (z % 2), 2 - z // 2, 3 * (1 - z // 2)][j]

    def gradient_step(t, j):
        corner = (t, j) not in CORNER_LATER
        if t not in ready:
            ready.append(t)
            all_dpre(t)
        all_pieces(t, nearest(j), corner)
        gradient(t, nearest(j), corner)

    for copy in load_pool:
        copy.start()
    load_w.start()
    pack()
    for t in range(TASKS):
        pre[t] = jnp.broadcast_to(bias[t:t + 1, :], (rows, cols))
    ends = LAYERS - 1
    pl.semaphore_wait(barrier, 4 + (z + ends - 1) // ends + (2 * ends - 1 - z) // ends)
    steps = {
        "places": places, "own": own_step, "layer": z_step, "share": square_sends, "forward": forward,
        "activate": activate_step, "core_terms": core_step, "chain": chain_step, "square": square_step,
        "corner": corner_step, "dpre": forward_dpre, "mixed": mixed_step, "gradient": gradient_step,
    }
    loaded = False
    for name, *which in ORDER:
        if name == "forward" and not loaded:
            load_w.wait()
            loaded = True
        steps[name](*which)
    for t, j in CORNER_LATER:
        corner_pieces(t, nearest(j))
    for layer in range(LAYERS):
        arrived(mg.at[layer * 2 + 1 - c], mc_r.at[layer])
    arrived(stv.at[bx], st_r.at[0])
    arrived(stv.at[by], st_r.at[1])
    arrived(stv.at[bd], st_r.at[2])
    for name in list(lent):
        give_back(name)
    for drain in drains:
        drain()
    st[...] = stv[...]
    at[0] = z // (LAYERS // 2)
    at[1] = bd
    at[2] = (jnp.max(stv[:, 6, :]) > rows).astype(jnp.int32)


def run_exchange(pool_in, weights, bias, stitch, crops, mask, first, cotangent, rows):
    tasks, slots, depth = pool_in.shape
    cols = weights.shape[2]
    parts = weights.shape[1] // depth
    sem = pltpu.SemaphoreType.DMA
    any_spec = pl.BlockSpec(memory_space=pl.ANY)
    vmem_spec = pl.BlockSpec(memory_space=pltpu.VMEM)
    two, four = TASKS, LAYERS
    piece = (rows, depth)
    return pl.pallas_call(
        exchange,
        out_shape=(
            jax.ShapeDtypeStruct((parts, tasks, GROUP * rows, depth), BF16),
            jax.ShapeDtypeStruct((tasks, GROUP * rows, cols), BF16),
            jax.ShapeDtypeStruct((parts, tasks, rows, cols), BF16),
            jax.ShapeDtypeStruct((tasks, rows, depth), BF16),
            jax.ShapeDtypeStruct((GROUP, 8, cols), F32),
            jax.ShapeDtypeStruct((slots, rows), BF16),
            jax.ShapeDtypeStruct((tasks, parts, cols, depth), BF16),
            jax.ShapeDtypeStruct((3,), jnp.int32),
        ),
        in_specs=[any_spec, any_spec] + [vmem_spec] * 6,
        out_specs=(any_spec, any_spec, any_spec, any_spec, vmem_spec, vmem_spec, any_spec, pl.BlockSpec(memory_space=pltpu.SMEM)),
        scratch_shapes=[
            pltpu.VMEM(weights.shape, BF16),
            pltpu.VMEM((tasks, rows, cols), F32),
            pltpu.VMEM((tasks, rows, cols), BF16),
            pltpu.VMEM((tasks, rows, cols), BF16),
            pltpu.VMEM((2, GROUP * rows, depth), BF16),
            pltpu.VMEM((tasks, *piece), BF16),
            pltpu.VMEM((tasks, rows, cols), BF16),
            pltpu.VMEM((GROUP * rows, cols), BF16),
            pltpu.VMEM((cols, GROUP * rows), BF16),
            pltpu.VMEM((2, cols, depth), BF16),
            pltpu.VMEM((rows, 1), F32),
            pltpu.VMEM((rows, depth // 3), F32),
            pltpu.VMEM((LAYERS, *piece), BF16),
            pltpu.VMEM((tasks, LAYERS - 1, *piece), BF16),
            pltpu.VMEM((tasks, LAYERS - 1, *piece), BF16),
            pltpu.VMEM((LAYERS, *piece), BF16),
            pltpu.VMEM((tasks, LAYERS, *piece), BF16),
            pltpu.VMEM((GROUP, 8, cols), F32),
            sem, sem((2 * GROUP,)), sem((two,)),
            sem((two, four)), sem((two, four)), sem((two, four)),
            sem((two, four)), sem((two, four)), sem((two, four)), sem((two, four)), sem((two, four)),
            sem((two, four)), sem((4, two, four)), sem((4, two, four)),
            sem((two, 4)), sem((two, 3)),
            sem((four,)), sem((four,)), sem((four,)), sem((four,)), sem((four + 1,)),
            sem((two, four)), sem((two, four)), sem((two, four)), sem((two, four)), sem((two, four)),
            sem((3,)), sem((3,)), sem((two,)), sem((2,)), sem((two, four)), sem((two, four)), sem((two, four)), sem((two, four)),
        ],
        compiler_params=pltpu.CompilerParams(
            collective_id=0, has_side_effects=True, vmem_limit_bytes=60 * 1024 * 1024),
        cost_estimate=pl.CostEstimate(
            flops=8 * tasks * rows * parts * depth * cols, bytes_accessed=150_000_000, transcendentals=0),
    )(pool_in, weights, bias, stitch, crops, mask, first, cotangent)


def block_of(p, at):
    half = pl.num_programs(0) // 2
    return p // 2 + half * ((at[0] + p % 2) % 2)


def finish(count, at, *refs):
    ins, (mixed, input_grad, weight_grad, bias_grad, stitch_grad, eye) = refs[:8 * count], refs[8 * count:]
    late = pl.program_id(0) % 2 == 1
    side = eye.shape[0]

    @pl.when(pl.program_id(0) == 0)
    def _():
        same = lax.broadcasted_iota(jnp.int32, eye.shape, 0) == lax.broadcasted_iota(jnp.int32, eye.shape, 1)
        eye[...] = jnp.where(same, 1.0, 0.0).astype(BF16)
        small = sum(jnp.sum(ins[8 * k + 7][...], axis=0) for k in range(count))
        bias_grad[...] = small[4:6, :]
        for t in range(TASKS):
            stitch_grad[t] = small[2 * t:2 * t + 2, :]

    for k in range(count):
        xg, dg, mg, ig, place, some, wg, st = ins[8 * k:8 * k + 8]
        depth = wg.shape[3]

        def put(ref, at, value):
            if k == 0:
                ref[at] = value.astype(ref.dtype)
            else:
                ref[at] += value.astype(ref.dtype)

        for t in range(TASKS):
            for low in range(0, depth, side):
                part = slice(low, min(low + side, depth))
                size = part.stop - low
                put(weight_grad, (t, part), lax.dot_general(
                    eye[0:size, 0:size], wg[t, 0, :, part], (((1,), (1,)), ((), ())), preferred_element_type=F32))

        @pl.when(late)
        def _():
            weight_grad[1] += lax.dot_general(
                xg[0, 0], dg[0], (((0,), (0,)), ((), ())), preferred_element_type=F32)

        for t in range(TASKS):
            put(mixed, t, jnp.dot(place[...], mg[0, t], preferred_element_type=F32))
            put(input_grad, t, jnp.dot(some[...], ig[t], preferred_element_type=F32))


def run_finish(passes):
    xg, dg, mg, ig, st, place, wg, at = passes[0]
    slots, rows = place.shape
    parts, tasks, all_rows, depth = xg.shape
    cols = dg.shape[2]
    some = slots // parts
    in_specs = [
        pl.BlockSpec((1, 1, rows, depth), lambda p, at: (p // 2 + parts // 2 * ((at[0] + 1) % 2), 1, at[1], 0)),
        pl.BlockSpec((1, rows, cols), lambda p, at: (1, at[1], 0)),
        pl.BlockSpec((1, tasks, rows, cols), lambda p, at: (block_of(p, at), 0, 0, 0)),
        pl.BlockSpec((tasks, rows, depth), lambda p, at: (0, 0, 0)),
        pl.BlockSpec((slots, rows), lambda p, at: (0, 0)),
        pl.BlockSpec((some, rows), lambda p, at: (p, 0)),
        pl.BlockSpec((tasks, 1, cols, depth), lambda p, at: (0, block_of(p, at), 0, 0)),
        pl.BlockSpec(st.shape, lambda p, at: (0, 0, 0)),
    ]
    flops = 2 * tasks * parts * cols * (rows * depth // 4 + slots * rows)
    return pl.pallas_call(
        functools.partial(finish, len(passes)),
        grid_spec=pltpu.PrefetchScalarGridSpec(
            num_scalar_prefetch=1,
            grid=(parts,),
            in_specs=in_specs * len(passes),
            out_specs=(
                pl.BlockSpec((tasks, slots, cols), lambda p, at: (0, 0, block_of(p, at))),
                pl.BlockSpec((tasks, some, depth), lambda p, at: (0, p, 0)),
                pl.BlockSpec((tasks, depth, cols), lambda p, at: (0, block_of(p, at), 0)),
                pl.BlockSpec((tasks, cols), lambda p, at: (0, 0)),
                pl.BlockSpec((tasks, tasks, cols), lambda p, at: (0, 0, 0)),
            ),
            scratch_shapes=[pltpu.VMEM((256, 256), BF16)],
        ),
        out_shape=(
            jax.ShapeDtypeStruct((tasks, slots, parts * cols), BF16),
            jax.ShapeDtypeStruct((tasks, slots, depth), BF16),
            jax.ShapeDtypeStruct((tasks, parts * depth, cols), F32),
            jax.ShapeDtypeStruct((tasks, cols), F32),
            jax.ShapeDtypeStruct((tasks, tasks, cols), F32),
        ),
        compiler_params=pltpu.CompilerParams(vmem_limit_bytes=60 * 1024 * 1024),
        cost_estimate=pl.CostEstimate(flops=flops, bytes_accessed=75_000_000, transcendentals=0),
    )(at, *[v for out in passes for v in (*out[:4], out[5], out[5], out[6], out[4])])


def packed_body(pool_in, weights, bias, stitch, crops, row_mask, cotangent):
    slots = row_mask.shape[0]
    rows = (slots * 17 // 32 + 15) // 16 * 16

    def part(first):
        return run_exchange(pool_in, weights, bias, stitch, crops.reshape(1, -1), row_mask.reshape(1, -1),
                            jnp.full((1, 1), first, jnp.int32), cotangent, rows)

    front = part(0)
    more = front[7][2] > 0
    return lax.cond(more, lambda: run_finish([front, part(rows)]), lambda: run_finish([front]))


def plain_body(pool_in, weights, bias, stitch, crops, row_mask, cotangent):
    hp = lax.Precision.HIGHEST
    count, valid = row_weights(crops, row_mask)
    features = lax.all_gather(pool_in, "mp", axis=2, tiled=True)
    linear = jnp.einsum("trk,tkc->trc", features, weights, preferred_element_type=jnp.float32)
    pre = linear + bias[:, None, :]
    hidden, gelu_back = jax.vjp(jax.nn.gelu, pre)
    stitched = stitch[:, 0, None, :] * hidden[0][None] + stitch[:, 1, None, :] * hidden[1][None]
    local_mixed = (valid[None, :, None] * stitched).astype(jnp.bfloat16)
    mixed = lax.all_gather(local_mixed, "mp", axis=2, tiled=True)
    scaled = valid[None, :, None] * cotangent.astype(jnp.float32) / count[None, :, None]
    stitch_part = jnp.einsum("trc,urc->tuc", scaled, hidden, precision=hp)
    through = jnp.einsum("tuc,trc->urc", stitch, scaled, precision=hp)
    dpre = gelu_back(through)[0].astype(jnp.bfloat16)
    bias_part = jnp.sum(dpre.astype(jnp.float32), axis=1)
    weight_part = jnp.einsum("trk,trc->tkc", features, dpre, preferred_element_type=jnp.float32)
    terms = jnp.einsum("trc,tkc->trk", dpre, weights, preferred_element_type=jnp.float32)
    input_sum = lax.psum_scatter(terms, "mp", scatter_dimension=2, tiled=True)
    weight_grad, bias_grad, stitch_grad = lax.psum((weight_part, bias_part, stitch_part), "batch")
    return (mixed, input_sum.astype(jnp.bfloat16), weight_grad, bias_grad, stitch_grad)


def solution(mesh):
    square = mesh.shape["batch"] == GROUP and mesh.shape["mp"] == 2 * LAYERS
    return jax.shard_map(
        packed_body if square else plain_body,
        mesh=mesh,
        in_specs=(
            P(None, "batch", "mp"),
            P(None, None, "mp"),
            P(None, "mp"),
            P(None, None, "mp"),
            P("batch"),
            P("batch"),
            P(None, "batch", "mp"),
        ),
        out_specs=(
            P(None, "batch", None),
            P(None, "batch", "mp"),
            P(None, None, "mp"),
            P(None, "mp"),
            P(None, None, "mp"),
        ),
        check_vma=False,
    )
```

profile of v0, /device:TPU:8, one launch (start us, length us, event | category | flops | bytes accessed | tf_op | source)
XLA Modules:
  0.0 228.8 jit_solution(14154545544192440670)
XLA Ops:
  0.6 0.0 copy-start
  0.6 0.0 copy-start.1
  0.7 0.0 copy-start.2
  0.7 0.0 copy-start.3
  0.7 195.7 %shard_map.120 = (bf16[8,2,1088,1152]{3,2,1,0:T(8,128)(2,1)}, bf16[2,1088,512]{2,1,0:T(8,128)(2,1)S(1)}, bf16[8,2,272,512]{3,2,1,0:T(8,128)(2,1)}, bf16[2,272,11...) custom-call(bf16[2,512,1152]{2,1,0:T(8,128)(2,1)} %pool.1, ...), custom_call_target="tpu_custom_call" | custom-call | flops 20535312384 | bytes 150000000 | tf_op jit(solution)/shard_map/pallas_call | solution.py:535
  196.4 0.6 slice.3
  197.7 0.0 copy-done
  197.7 0.0 copy-done.1
  197.7 0.0 copy-done.2
  197.7 0.0 copy-done.3
  197.7 30.9 %conditional.1 = ((bf16[2,512,4096]{2,1,0:T(8,128)(2,1)}, bf16[2,512,1152]{2,1,0:T(8,128)(2,1)}, f32[2,9216,512]{2,1,0:T(8,128)}, f32[2,512]{1,0:T(2,128)}, f32[2,2,512]{2,1,0:T(2,128)})) conditional(s32[]{:T(128)} %bitcast.4, (s32[3]{0:T(128)S(1)}, bf16[8,2,1088,1152]{3,2,1,0:T(8,128)(2,1)}, bf16[2,1088,512]{2,1,0:T(8,128)(2,1)S(1)}, ...), branch_computations={%region_0.0_spmd, %region_1.0_spmd} | conditional | flops 24100470784 | bytes 225000000 | solution.py:684
  197.7 30.6 %branch_0_fun.1 = (bf16[2,512,4096]{2,1,0:T(8,128)(2,1)}, bf16[2,512,1152]{2,1,0:T(8,128)(2,1)}, f32[2,9216,512]{2,1,0:T(8,128)}, f32[2,512]{1,0:T(2,128)}, f32[2,2,512]{2,1,0:T(2,128)}) custom-call(s32[3]{0:T(128)S(1)} %get-tuple-element.46.at, bf16[8,2,1088,1152]{3,2,1,0:T(8,128)(2,1)} %get-tuple-element.47.refs_0_, ...), custom_call_target="tpu_custom_call" | custom-call | flops 3565158400 | bytes 75000000 | tf_op jit(solution)/shard_map/cond/branch_0_fun/pallas_call | solution.py:647
Async XLA Ops:
  0.6 197.0 %copy-start = (f32[2,2,512]{2,1,0:T(2,128)S(1)}, f32[2,2,512]{2,1,0:T(2,128)}, u32[]{:S(2)}) copy-start(f32[2,2,512]{2,1,0:T(2,128)} %stitch.1) | copy-start | bytes 24580
  0.6 197.0 %copy-start.1 = (f32[2,512]{1,0:T(2,128)S(1)}, f32[2,512]{1,0:T(2,128)}, u32[]{:S(2)}) copy-start(f32[2,512]{1,0:T(2,128)} %bias.1) | copy-start | bytes 12292
  0.7 197.0 %copy-start.2 = (s32[512]{0:T(512)S(1)}, s32[512]{0:T(512)}, u32[]{:S(2)}) copy-start(s32[512]{0:T(512)} %param.14) | copy-start | bytes 6148
  0.7 197.0 %copy-start.3 = (s32[128]{0:T(128)S(1)}, s32[128]{0:T(128)}, u32[]{:S(2)}) copy-start(s32[128]{0:T(128)} %param.13) | copy-start | bytes 1540
where the time goes:
time: 229 us
  Pallas kernels  226 us (99%)
    pallas_call x1, Pallas kernels, run_exchange(): pl.pallas_call(exchange, out_shape=(jax.ShapeDtypeStruct((parts, tasks, G...  196 us
    pallas_call x1, Pallas kernels, run_finish(): pl.pallas_call(functools.partial(finish, len(passes)), grid_spec=pltpu.Pr...  30.6 us

commit v1 on v0

--- a/solution.py
+++ b/solution.py
@@ -49,7 +49,7 @@
 
 
 def exchange(pool, w, bias, stitch, crops, mask, first, cotangent, xg, dg, mg, ig, st, place, wg, at,
-             wv, pre, dpv, mxv, gx, xc, cot, dgv, dgt, gout, scale, acc, sbuf, rup, rdn, tso, tsi, stv,
+             wv, pre, dpv, mxv, gx, xc, cot, picked, dgv, dgt, gout, scale, acc, sbuf, rup, rdn, tso, tsi, stv,
              wsem, lsem, osem, z_r, z_u, z_d, o_x, o_y, r_x, r_y, r_d, f_s, c_r, c_s,
              dp_s, dp_r, m_r, m_u, m_d, mc_r, mc_s, t_u, t_d, t_s, tc_r, tc_s, st_s, st_r, ig_s, go_s, v_u, v_d, f_h, r_h):
     rows, depth = xc.shape[1], xc.shape[2]
@@ -145,11 +145,18 @@
         stv[b, 6:7, :] = jnp.broadcast_to(jnp.sum(valid, axis=1, keepdims=True), (1, cols))
         stv[b, 7:8, :] = jnp.zeros((1, cols), F32)
         pick = pick.astype(BF16)
+        picked[...] = pick
+        pack_task(0)
+
+    def pack_task(t):
+        load_pool[t].wait()
+        xc[t] = jnp.dot(picked[...], gx[t, 0:slots, :], preferred_element_type=F32).astype(BF16)
+
+    def pack_rest():
+        pack_task(1)
         for t in range(TASKS):
-            load_pool[t].wait()
-            xc[t] = jnp.dot(pick, gx[t, 0:slots, :], preferred_element_type=F32).astype(BF16)
-        for t in range(TASKS):
-            cot[t] = jnp.dot(pick, cotangent[t], preferred_element_type=F32).astype(BF16)
+            cot[t] = jnp.dot(picked[...], cotangent[t], preferred_element_type=F32).astype(BF16)
+            pre[t] = jnp.broadcast_to(bias[t:t + 1, :], (rows, cols))
 
     def places():
         valid, _ = row_weights()
@@ -491,8 +498,6 @@
         copy.start()
     load_w.start()
     pack()
-    for t in range(TASKS):
-        pre[t] = jnp.broadcast_to(bias[t:t + 1, :], (rows, cols))
     ends = LAYERS - 1
     pl.semaphore_wait(barrier, 4 + (z + ends - 1) // ends + (2 * ends - 1 - z) // ends)
     steps = {
@@ -500,8 +505,11 @@
         "activate": activate_step, "core_terms": core_step, "chain": chain_step, "square": square_step,
         "corner": corner_step, "dpre": forward_dpre, "mixed": mixed_step, "gradient": gradient_step,
     }
-    loaded = False
+    loaded = packed = False
     for name, *which in ORDER:
+        if not packed and (name, *which) not in (("own", 0), ("share", 0, 0)):
+            pack_rest()
+            packed = True
         if name == "forward" and not loaded:
             load_w.wait()
             loaded = True
@@ -554,6 +562,7 @@
             pltpu.VMEM((2, GROUP * rows, depth), BF16),
             pltpu.VMEM((tasks, *piece), BF16),
             pltpu.VMEM((tasks, rows, cols), BF16),
+            pltpu.VMEM((rows, slots), BF16),
             pltpu.VMEM((GROUP * rows, cols), BF16),
             pltpu.VMEM((cols, GROUP * rows), BF16),
             pltpu.VMEM((2, cols, depth), BF16),
@@ -610,12 +619,12 @@
             else:
                 ref[at] += value.astype(ref.dtype)
 
-        for t in range(TASKS):
-            for low in range(0, depth, side):
-                part = slice(low, min(low + side, depth))
-                size = part.stop - low
-                put(weight_grad, (t, part), lax.dot_general(
-                    eye[0:size, 0:size], wg[t, 0, :, part], (((1,), (1,)), ((), ())), preferred_element_type=F32))
+        put(weight_grad, 0, wg[0, 0].T.astype(F32))
+        for low in range(0, depth, side):
+            part = slice(low, min(low + side, depth))
+            size = part.stop - low
+            put(weight_grad, (1, part), lax.dot_general(
+                eye[0:size, 0:size], wg[1, 0, :, part], (((1,), (1,)), ((), ())), preferred_element_type=F32))
 
         @pl.when(late)
         def _():

time: 229 us -> 227 us (level)
  no operation moved by 1% of the time
where the time goes in v1:
time: 227 us
  Pallas kernels  224 us (99%)
    pallas_call x1, Pallas kernels, run_exchange(): pl.pallas_call(exchange, out_shape=(jax.ShapeDtypeStruct((parts, tasks, G...  195 us
    pallas_call x1, Pallas kernels, run_finish(): pl.pallas_call(functools.partial(finish, len(passes)), grid_spec=pltpu.Pr...  29.5 us

profile of v1, /device:TPU:8, one launch (start us, length us, event | category | flops | bytes accessed | tf_op | source)
XLA Modules:
  0.0 226.7 jit_solution(1420272590786010235)
XLA Ops:
  0.6 0.0 copy-start
  0.6 0.0 copy-start.1
  0.7 0.0 copy-start.2
  0.7 0.0 copy-start.3
  0.7 194.8 %shard_map.120 = (bf16[8,2,1088,1152]{3,2,1,0:T(8,128)(2,1)}, bf16[2,1088,512]{2,1,0:T(8,128)(2,1)S(1)}, bf16[8,2,272,512]{3,2,1,0:T(8,128)(2,1)}, bf16[2,272,11...) custom-call(bf16[2,512,1152]{2,1,0:T(8,128)(2,1)} %pool.1, ...), custom_call_target="tpu_custom_call" | custom-call | flops 20535312384 | bytes 150000000 | tf_op jit(solution)/shard_map/pallas_call | solution.py:543
  195.5 0.6 slice.3
  196.7 0.0 copy-done
  196.7 0.0 copy-done.1
  196.7 0.0 copy-done.2
  196.7 0.0 copy-done.3
  196.7 29.7 %conditional.1 = ((bf16[2,512,4096]{2,1,0:T(8,128)(2,1)}, bf16[2,512,1152]{2,1,0:T(8,128)(2,1)}, f32[2,9216,512]{2,1,0:T(8,128)}, f32[2,512]{1,0:T(2,128)}, f32[2,2,512]{2,1,0:T(2,128)})) conditional(s32[]{:T(128)} %bitcast.4, (s32[3]{0:T(128)S(1)}, bf16[8,2,1088,1152]{3,2,1,0:T(8,128)(2,1)}, bf16[2,1088,512]{2,1,0:T(8,128)(2,1)S(1)}, ...), branch_computations={%region_0.0_spmd, %region_1.0_spmd} | conditional | flops 24100470784 | bytes 225000000 | solution.py:693
  196.8 29.5 %branch_0_fun.1 = (bf16[2,512,4096]{2,1,0:T(8,128)(2,1)}, bf16[2,512,1152]{2,1,0:T(8,128)(2,1)}, f32[2,9216,512]{2,1,0:T(8,128)}, f32[2,512]{1,0:T(2,128)}, f32[2,2,512]{2,1,0:T(2,128)}) custom-call(s32[3]{0:T(128)S(1)} %get-tuple-element.46.at, bf16[8,2,1088,1152]{3,2,1,0:T(8,128)(2,1)} %get-tuple-element.47.refs_0_, ...), custom_call_target="tpu_custom_call" | custom-call | flops 3565158400 | bytes 75000000 | tf_op jit(solution)/shard_map/cond/branch_0_fun/pallas_call | solution.py:656
Async XLA Ops:
  0.6 196.1 %copy-start = (f32[2,2,512]{2,1,0:T(2,128)S(1)}, f32[2,2,512]{2,1,0:T(2,128)}, u32[]{:S(2)}) copy-start(f32[2,2,512]{2,1,0:T(2,128)} %stitch.1) | copy-start | bytes 24580
  0.6 196.1 %copy-start.1 = (f32[2,512]{1,0:T(2,128)S(1)}, f32[2,512]{1,0:T(2,128)}, u32[]{:S(2)}) copy-start(f32[2,512]{1,0:T(2,128)} %bias.1) | copy-start | bytes 12292
  0.7 196.1 %copy-start.2 = (s32[512]{0:T(512)S(1)}, s32[512]{0:T(512)}, u32[]{:S(2)}) copy-start(s32[512]{0:T(512)} %param.14) | copy-start | bytes 6148
  0.7 196.1 %copy-start.3 = (s32[128]{0:T(128)S(1)}, s32[128]{0:T(128)}, u32[]{:S(2)}) copy-start(s32[128]{0:T(128)} %param.13) | copy-start | bytes 1540
